TPU v7x, 256 devices: a whole 4x4x8 slice. The times are simulated.
256 devices in a mesh: seq: 32 (over y, z), head: 8 (over x, core).
Axes of the slice: x: 4, y: 4, z: 8, core: 2. Of those that a mesh axis runs over, the one named last changes fastest.
Arguments:
- queries: bfloat16 [32768, 32, 128], P('seq', 'head'), may hold values from -6 to 6
- key_rows: bfloat16 [32768, 32, 128], P('seq', 'head'), may hold values from -6 to 6
- value_rows: bfloat16 [32768, 32, 128], P('seq', 'head'), may hold values from -6 to 6
- out_grad: bfloat16 [32768, 4096], P('seq', 'head'), may hold values from -6 to 6
- out_weight: bfloat16 [32, 128, 4096], P('head'), may hold values from -0.09375 to 0.09375
Outputs:
- query_grad: bfloat16 [32768, 32, 128], P('seq', 'head')
- key_grad: bfloat16 [32768, 32, 128], P('seq', 'head')
- value_grad: bfloat16 [32768, 32, 128], P('seq', 'head')
All inputs are finite; a program needn't handle non-finite values.
Results may differ from a plain program's by a relative error of at most 0.0058.
Values may be sent and summed in bfloat16 or wider, within the bound.
No kernel may reach another device: no remote copies, remote signals or barrier semaphores. Data moves between devices by JAX's collectives and lax.ppermute only.
A program may use at most 128 MiB of HBM per device.

v0:
```python
import math
import jax
import jax.numpy as jnp
from jax import lax
from jax.sharding import PartitionSpec as P

BLOCK = 256


def body(queries, key_rows, value_rows, out_grad, out_weight):
    tokens = queries.shape[0]
    heads = queries.shape[1]
    depth = queries.shape[2]
    blocks = tokens // BLOCK
    factor = 1.0 / math.sqrt(depth * tokens * lax.axis_size("seq"))
    attn_grad = jnp.einsum(
        "tm,hdm->thd",
        lax.all_gather(out_grad, "head", axis=1, tiled=True),
        out_weight,
        preferred_element_type=jnp.float32,
    ).astype(jnp.bfloat16)
    layout = (blocks, BLOCK, heads, depth)
    query_blocks = queries.reshape(layout)
    key_blocks = key_rows.reshape(layout)
    value_blocks = value_rows.reshape(layout)
    grad_blocks = attn_grad.reshape(layout)
    kv_parts = jnp.einsum(
        "bthd,bthe->bhde", key_blocks, value_blocks, preferred_element_type=jnp.float32
    )
    qg_parts = jnp.einsum(
        "bthd,bthe->bhde", query_blocks, grad_blocks, preferred_element_type=jnp.float32
    )
    kv_total = jnp.sum(kv_parts, 0)
    qg_total = jnp.sum(qg_parts, 0)
    shards = lax.axis_size("seq")
    stacked = jnp.stack([kv_total, qg_total]).reshape(2, shards, -1)
    pieces = lax.all_to_all(stacked, "seq", split_axis=1, concat_axis=1, tiled=True)
    forward_sums = jnp.cumsum(pieces[0], 0) - pieces[0]
    reverse_sums = jnp.cumsum(pieces[1][::-1], 0)[::-1] - pieces[1]
    totals = lax.all_to_all(
        jnp.stack([forward_sums, reverse_sums]), "seq", split_axis=1, concat_axis=1, tiled=True
    )
    totals = totals.reshape(2, heads, depth, depth)
    before = totals[0]
    after = totals[1]
    first_zero = jnp.zeros((1, heads, depth, depth), jnp.float32)
    running = jnp.cumsum(kv_parts, 0)
    prefix = before[None] + jnp.concatenate([first_zero, running[:-1]], 0)
    backward_sums = jnp.cumsum(qg_parts[::-1], 0)[::-1]
    suffix = after[None] + jnp.concatenate([backward_sums[1:], first_zero], 0)
    prefix_bf = prefix.astype(jnp.bfloat16)
    suffix_bf = suffix.astype(jnp.bfloat16)
    causal = jnp.tril(jnp.ones((BLOCK, BLOCK), bool))
    qk_scores = jnp.einsum(
        "bthd,bshd->bhts", query_blocks, key_blocks, preferred_element_type=jnp.float32
    )
    qk_scores = jnp.where(causal, qk_scores, 0.0).astype(jnp.bfloat16)
    grad_scores = jnp.einsum(
        "bthd,bshd->bhts", grad_blocks, value_blocks, preferred_element_type=jnp.float32
    )
    grad_scores = jnp.where(causal, grad_scores, 0.0).astype(jnp.bfloat16)
    query_grad = jnp.einsum(
        "bhts,bshd->bthd", grad_scores, key_blocks, preferred_element_type=jnp.float32
    )
    query_grad = query_grad + jnp.einsum(
        "bthe,bhde->bthd", grad_blocks, prefix_bf, preferred_element_type=jnp.float32
    )
    key_grad = jnp.einsum(
        "bhts,bthd->bshd", grad_scores, query_blocks, preferred_element_type=jnp.float32
    )
    key_grad = key_grad + jnp.einsum(
        "bshe,bhde->bshd", value_blocks, suffix_bf, preferred_element_type=jnp.float32
    )
    value_grad = jnp.einsum(
        "bhts,bthe->bshe", qk_scores, grad_blocks, preferred_element_type=jnp.float32
    )
    value_grad = value_grad + jnp.einsum(
        "bshd,bhde->bshe", key_blocks, suffix_bf, preferred_element_type=jnp.float32
    )
    final_shape = (tokens, heads, depth)
    return (
        (factor * query_grad).astype(jnp.bfloat16).reshape(final_shape),
        (factor * key_grad).astype(jnp.bfloat16).reshape(final_shape),
        (factor * value_grad).astype(jnp.bfloat16).reshape(final_shape),
    )


def solution(mesh):
    placed = (
        P("seq", "head", None),
        P("seq", "head", None),
        P("seq", "head", None),
        P("seq", "head"),
        P("head", None, None),
    )
    return jax.shard_map(
        body,
        mesh=mesh,
        in_specs=placed,
        out_specs=(P("seq", "head", None), P("seq", "head", None), P("seq", "head", None)),
        check_vma=False,
    )
```

profile of v0, /device:TPU:32, one launch (start us, length us, event | category | flops | bytes accessed | tf_op | source)
XLA Modules:
  0.0 155.0 jit_solution(7390798430991049583)
XLA Ops:
  7.9 2.1 %fusion.38 = (f32[4,128,128]{2,1,0:T(8,128)S(1)}, f32[4,4,128,128]{3,2,1,0:T(8,128)S(1)}) fusion(bf16[4,256,4,128]{3,2,1,0:T(4,128)(2,1)} %bitcast.53, bf16[4,256,4,128]{3,2,1,0:T(4,128)(2,1)} %bitcast.46), kind=kOutput, calls=%fused_computation.48 | convolution fusion | flops 134414336 | bytes 3407872 | tf_op jit(solution)/shard_map/bthd,bthe->bhde/dot_general | solution.py:27
  10.0 54.7 %all-gather.2.cloned.1.call-done = bf16[1024,4096]{1,0:T(8,128)(2,1)} async-done(((bf16[1024,512]{1,0:T(8,128)(2,1)}), bf16[1024,4096]{1,0:T(8,128)(2,1)}) %all-gather.2.cloned.1.call-update) | async-done | bytes 8388624 | tf_op jit(solution)/shard_map/all_gather | solution.py:18
  64.7 8.2 %fusion.7 = bf16[1024,4,128]{2,0,1:T(8,128)(2,1)S(1)} fusion(bf16[4,128,4096]{2,1,0:T(8,128)(2,1)} %param.9, bf16[1024,4096]{1,0:T(8,128)(2,1)} %all-gather.2.cloned.1.call-done), kind=kOutput, calls=%fused_computation.12 | convolution fusion | flops 4295491584 | bytes 13631488 | tf_op jit(solution)/shard_map/tm,hdm->thd/dot_general | solution.py:16
  73.0 1.2 fusion.37
  74.2 1.1 copy.83
  75.4 1.2 copy.84
  76.6 10.1 %all-to-all-start = ((f32[2,32,2048]{2,0,1:T(2,128)}), f32[2,32,2048]{2,0,1:T(2,128)}, u32[]{:S(2)}, u32[]{:S(2)}) async-start(f32[2,32,2048]{2,0,1:T(2,128)} %copy.84), calls=%async_computation | async-start | bytes 1048576 | tf_op jit(solution)/shard_map/all_to_all | solution.py:37
  87.6 1.0 copy-done.9
  89.5 0.9 slice.31
  90.9 1.9 %select_convert_fusion.1 = bf16[4,4,256,256]{3,2,1,0:T(8,128)(2,1)S(1)} fusion(pred[256,256]{1,0:T(8,128)(4,1)S(1)} %iota_compare_fusion, bf16[4,256,4,128]{3,2,1,0:T(4,128)(2,1)S(1)} %bitcast.54, bf16[4,256,4,128]{3,1,0,2:T(8,128)(2,1)} %bitcast.57), kind=kOutput, calls=%fused_computation.3 | convolution fusion | flops 270532608 | bytes 4259840 | tf_op jit(solution)/shard_map/bthd,bshd->bhts/dot_general | solution.py:58
  92.9 12.0 %all-to-all-done = f32[2,32,2048]{2,0,1:T(2,128)} async-done(((f32[2,32,2048]{2,0,1:T(2,128)}), f32[2,32,2048]{2,0,1:T(2,128)}, u32[]{:S(2)}, u32[]{:S(2)}) %all-to-all-start) | async-done | bytes 524320 | tf_op jit(solution)/shard_map/all_to_all | solution.py:37
  104.9 1.7 %fusion.36 = (f32[1,32,2048]{2,0,1:T(1,128)S(1)}, f32[1,32,2048]{2,0,1:T(1,128)S(1)}) fusion(f32[2,32,2048]{2,0,1:T(2,128)} %all-to-all-done), kind=kLoop, calls=%fused_computation.46 | loop fusion | bytes 1048576 | tf_op jit(solution)/shard_map/slice | solution.py:38
  108.1 1.2 copy.87
  109.3 4.9 %all-to-all-start.1 = ((f32[2,32,2048]{2,0,1:T(2,128)}), f32[2,32,2048]{2,0,1:T(2,128)}, u32[]{:S(2)}, u32[]{:S(2)}) async-start(f32[2,32,2048]{2,0,1:T(2,128)} %copy.87), calls=%async_computation.1 | async-start | bytes 1048576 | tf_op jit(solution)/shard_map/all_to_all | solution.py:40
  114.2 3.4 %fusion.13 = f32[4,4,256,128]{3,2,1,0:T(8,128)} fusion(bf16[4,4,256,256]{3,2,1,0:T(8,128)(2,1)S(1)} %select_convert_fusion.1, bf16[4,256,4,128]{3,2,1,0:T(4,128)(2,1)} %bitcast.50), kind=kOutput, calls=%fused_computation.18 | convolution fusion | flops 268435456 | bytes 5242880 | tf_op jit(solution)/shard_map/bhts,bthd->bshd/dot_general | solution.py:68
  117.6 2.0 %fusion.24 = f32[4,4,256,128]{3,2,1,0:T(8,128)} fusion(bf16[4,4,256,256]{3,2,1,0:T(8,128)(2,1)S(1)} %select_convert_fusion.1, bf16[4,256,4,128]{3,2,1,0:T(4,128)(2,1)S(1)} %bitcast.47), kind=kOutput, calls=%fused_computation.28 | convolution fusion | flops 268435456 | bytes 5242880 | tf_op jit(solution)/shard_map/bhts,bshd->bthd/dot_general | solution.py:62
  119.7 3.9 %fusion.6 = f32[4,4,128,256]{3,2,1,0:T(8,128)} fusion(pred[256,256]{1,0:T(8,128)(4,1)S(1)} %iota_compare_fusion, bf16[4,256,4,128]{3,2,1,0:T(4,128)(2,1)} %bitcast.51, bf16[4,256,4,128]{3,2,1,0:T(4,128)(2,1)S(1)} %bitcast.48, bf16[4,256,4,128]{3,1,0,2:T(8,128)(2,1)} %bitcast.58), kind=kOutput, calls=%fused_computation.11 | convolution fusion | flops 538968064 | bytes 5308416 | tf_op jit(solution)/shard_map/bhts,bthe->bshe/dot_general | solution.py:74
  123.6 8.1 %all-to-all-done.1 = f32[2,32,2048]{2,0,1:T(2,128)} async-done(((f32[2,32,2048]{2,0,1:T(2,128)}), f32[2,32,2048]{2,0,1:T(2,128)}, u32[]{:S(2)}, u32[]{:S(2)}) %all-to-all-start.1) | async-done | bytes 524320 | tf_op jit(solution)/shard_map/all_to_all | solution.py:40
  131.7 2.5 %fusion.35 = (f32[1,32,2048]{2,0,1:T(1,128)S(1)}, f32[1,32,2048]{2,0,1:T(1,128)}) fusion(f32[2,32,2048]{2,0,1:T(2,128)} %all-to-all-done.1), kind=kLoop, calls=%fused_computation.45 | loop fusion | bytes 1048576 | tf_op jit(solution)/shard_map/slice | solution.py:45
  134.3 3.0 %fusion.10 = bf16[4,256,4,128]{1,3,2,0:T(8,128)(2,1)} fusion(f32[4,4,128,256]{3,2,1,0:T(8,128)} %fusion.6, bf16[4,256,4,128]{3,2,1,0:T(4,128)(2,1)S(1)} %bitcast.49, f32[3,4,128,128]{2,3,1,0:T(8,128)S(1)} %copy-done.3, f32[4,128,128]{1,2,0:T(8,128)S(1)} %copy.93), kind=kOutput, calls=%fused_computation.13 | convolution fusion | flops 136314880 | bytes 5242880 | tf_op jit(solution)/shard_map/bshd,bhde->bshe/dot_general | solution.py:77
  137.3 2.4 %copy.102 = bf16[4,256,4,128]{3,1,0,2:T(8,128)(2,1)} copy(bf16[4,256,4,128]{1,3,2,0:T(8,128)(2,1)} %fusion.10) | data formatting | bytes 2097152 | tf_op jit(solution)/shard_map/convert_element_type | solution.py:84
  139.7 3.1 %copy.105 = bf16[1024,4,128]{2,1,0:T(4,128)(2,1)} copy(bf16[1024,4,128]{2,0,1:T(8,128)(2,1)} %bitcast.60) | data formatting | bytes 2097152
  143.5 1.8 %copy.104 = bf16[1024,4,128]{2,1,0:T(4,128)(2,1)} copy(bf16[1024,4,128]{2,0,1:T(8,128)(2,1)S(1)} %bitcast.61) | data formatting | bytes 2097152
  146.4 1.8 %copy.103 = bf16[1024,4,128]{2,1,0:T(4,128)(2,1)} copy(bf16[1024,4,128]{2,0,1:T(8,128)(2,1)S(1)} %bitcast.62) | data formatting | bytes 2097152
  (47 shorter events, 6.4 us)
Async XLA Ops:
  7.2 57.6 %all-gather.2.cloned.1.call-start = ((), (), s32[]{:S(2)}) async-start(), calls=%async_computation.2 | async-start | bytes 9437184 | tf_op jit(solution)/shard_map/all_gather | solution.py:18
  10.0 62.9 %copy-start.4 = (bf16[1024,4,128]{2,1,0:T(4,128)(2,1)S(1)}, bf16[1024,4,128]{2,1,0:T(4,128)(2,1)}, u32[]{:S(2)}) copy-start(bf16[1024,4,128]{2,1,0:T(4,128)(2,1)} %param.5) | copy-start | bytes 3145732
  72.9 1.3 copy-start.7
  76.6 28.3 %all-to-all-start = ((f32[2,32,2048]{2,0,1:T(2,128)}), f32[2,32,2048]{2,0,1:T(2,128)}, u32[]{:S(2)}, u32[]{:S(2)}) async-start(f32[2,32,2048]{2,0,1:T(2,128)} %copy.84), calls=%async_computation | async-start | bytes 1048576 | tf_op jit(solution)/shard_map/all_to_all | solution.py:37
  87.5 1.0 copy-start.9
  89.4 1.5 copy-start.5
  109.3 22.4 %all-to-all-start.1 = ((f32[2,32,2048]{2,0,1:T(2,128)}), f32[2,32,2048]{2,0,1:T(2,128)}, u32[]{:S(2)}, u32[]{:S(2)}) async-start(f32[2,32,2048]{2,0,1:T(2,128)} %copy.87), calls=%async_computation.1 | async-start | bytes 1048576 | tf_op jit(solution)/shard_map/all_to_all | solution.py:40
  114.2 3.4 %copy-start = (bf16[1024,4,128]{2,1,0:T(4,128)(2,1)S(1)}, bf16[1024,4,128]{2,1,0:T(4,128)(2,1)}, u32[]{:S(2)}) copy-start(bf16[1024,4,128]{2,1,0:T(4,128)(2,1)} %param.6) | copy-start | bytes 3145732
  123.6 10.7 %copy-start.3 = (f32[3,4,128,128]{2,3,1,0:T(8,128)S(1)}, f32[3,4,128,128]{2,3,1,0:T(8,128)}, u32[]{:S(2)}) copy-start(f32[3,4,128,128]{2,3,1,0:T(8,128)} %slice.31) | copy-start | bytes 2359300
  137.3 5.5 %copy-start.2 = (f32[4,4,256,128]{3,2,1,0:T(8,128)S(1)}, f32[4,4,256,128]{3,2,1,0:T(8,128)}, u32[]{:S(2)}) copy-start(f32[4,4,256,128]{3,2,1,0:T(8,128)} %fusion.13) | copy-start | bytes 6291460
  139.7 3.1 %copy-start.6 = (bf16[1024,4,128]{2,1,0:T(4,128)(2,1)S(1)}, bf16[1024,4,128]{2,1,0:T(4,128)(2,1)}, u32[]{:S(2)}) copy-start(bf16[1024,4,128]{2,1,0:T(4,128)(2,1)} %param.7) | copy-start | bytes 3145732
  143.3 1.9 %copy-start.1 = (f32[4,4,256,128]{3,2,1,0:T(8,128)S(1)}, f32[4,4,256,128]{3,2,1,0:T(8,128)}, u32[]{:S(2)}) copy-start(f32[4,4,256,128]{3,2,1,0:T(8,128)} %fusion.24) | copy-start | bytes 6291460
  143.3 1.9 %copy-start.8 = (bf16[1024,4,128]{2,0,1:T(8,128)(2,1)S(1)}, bf16[1024,4,128]{2,0,1:T(8,128)(2,1)}, u32[]{:S(2)}) copy-start(bf16[1024,4,128]{2,0,1:T(8,128)(2,1)} %copy-done.7) | copy-start | bytes 3145732
  143.3 2.4 %slice-start = ((f32[4,4,128,128]{3,2,1,0:T(8,128)}), f32[3,4,128,128]{3,2,1,0:T(8,128)S(1)}, s32[]{:S(2)}) async-start(f32[4,4,128,128]{3,2,1,0:T(8,128)} %copy-done.9), calls=%async_computation.3 | async-start | bytes 1572864 | tf_op jit(solution)/shard_map/slice | solution.py:48
  143.4 2.5 %copy-start.10 = (f32[1,32,2048]{2,0,1:T(1,128)S(1)}, f32[1,32,2048]{2,0,1:T(1,128)}, u32[]{:S(2)}) copy-start(f32[1,32,2048]{2,0,1:T(1,128)} %get-tuple-element.13) | copy-start | bytes 786436
Sparse Core Ops, SparseCore 0:
  9.8 54.8 all-gather.1
where the time goes:
time: 156 us; the launch traced here: 155 us
  waiting for transfers between devices  75.5 us (48%)
  matrix products  26.8 us (17%)
  local copies, waits for them, and re-layouts  21.1 us (14%)
  starting transfers between devices  15.1 us (10%)
  between operations  14.3 us (9%)
  other arithmetic  2.3 us (1%)
    all_gather x1, waiting for transfers between devices, body(): lax.all_gather(out_grad, 'head', axis=1, tiled=True)  54.7 us
    all_to_all x1, waiting for transfers between devices, body(): lax.all_to_all(stacked, 'seq', split_axis=1, concat_axis=1, tiled=True)  12 us
    all_to_all x1, starting transfers between devices, body(): lax.all_to_all(stacked, 'seq', split_axis=1, concat_axis=1, tiled=True)  10.1 us
    unnamed x27, local copies, waits for them, and re-layouts  8.39 us
    dot_general x1, matrix products, body(): jnp.einsum('tm,hdm->thd', lax.all_gather(out_grad, 'head', axis=1, tiled=...  8.22 us
    all_to_all x1, waiting for transfers between devices, body(): lax.all_to_all(jnp.stack([forward_sums, reverse_sums]), 'seq', split_axis...  8.12 us
    all_to_all x1, starting transfers between devices, body(): lax.all_to_all(jnp.stack([forward_sums, reverse_sums]), 'seq', split_axis...  4.9 us
    dot_general x1, matrix products, body(): jnp.einsum('bhts,bthe->bshe', qk_scores, grad_blocks, preferred_element_t...  3.89 us
  transfers between devices with their start and end apart: 3, of which 3 were waited for; matrix products, arithmetic and copies ran while one was open for 10% of the time, Pallas kernels for 0%

commit v1 on v0

--- a/solution.py
+++ b/solution.py
@@ -15,7 +15,9 @@
     factor = 1.0 / math.sqrt(depth * tokens * lax.axis_size("seq"))
     attn_grad = jnp.einsum(
         "tm,hdm->thd",
-        lax.all_gather(out_grad, "head", axis=1, tiled=True),
+        jnp.concatenate(
+            lax.all_to_all(jnp.stack([out_grad] * lax.axis_size("head")), "head", 0, 0), axis=1
+        ),
         out_weight,
         preferred_element_type=jnp.float32,
     ).astype(jnp.bfloat16)

time: 156 us -> 243 us (1.56)
  local copies, waits for them, and re-layouts: 21.1 us -> 69.4 us
  waiting for transfers between devices: 75.5 us -> 113 us
  between operations: 14.3 us -> 0.89 us
  other arithmetic: 2.3 us -> 10.2 us
  starting transfers between devices: 15.1 us -> 21.4 us
    all_to_all x0 -> x1, waiting for transfers between devices: none -> 93.3 us  [body(): lax.all_to_all(jnp.stack([out_grad] * lax.axis_size('head')), 'head', 0, 0)]
    all_gather x1 -> x0, waiting for transfers between devices: 54.7 us -> none  [body(): lax.all_gather(out_grad, 'head', axis=1, tiled=True)]
    reshape x0 -> x2, local copies, waits for them, and re-layouts: none -> 24.8 us  [body(): jnp.concatenate(lax.all_to_all(jnp.stack([out_grad] * lax.axis_size('head...]
    rev x2, local copies, waits for them, and re-layouts: 0.59 us -> 15.9 us  [body(): reverse_sums = jnp.cumsum(pieces[1][::-1], 0)[::-1] - pieces[1]]
    another operation x0 -> x1, local copies, waits for them, and re-layouts: none -> 5.17 us  [body(): jnp.stack([out_grad] * lax.axis_size('head'))]
    all_to_all x0 -> x1, starting transfers between devices: none -> 5.07 us  [body(): lax.all_to_all(jnp.stack([out_grad] * lax.axis_size('head')), 'head', 0, 0)]
    unnamed x27 -> x31, local copies, waits for them, and re-layouts: 8.39 us -> 9.97 us
  transfers between devices with their start and end apart: 3 -> 3, of which waited for: 3 -> 3; matrix products, arithmetic and copies ran while one was open for 10% -> 6% of each run, Pallas kernels for 0% -> 0%
where the time goes in v1:
time: 243 us; the launch traced here: 240 us
  waiting for transfers between devices  113 us (47%)
  local copies, waits for them, and re-layouts  69.4 us (29%)
  matrix products  25.5 us (10%)
  starting transfers between devices  21.4 us (9%)
  other arithmetic  10.2 us (4%)
    all_to_all x1, waiting for transfers between devices, body(): lax.all_to_all(jnp.stack([out_grad] * lax.axis_size('head')), 'head', 0, 0)  93.3 us
    reshape x2, local copies, waits for them, and re-layouts, body(): jnp.concatenate(lax.all_to_all(jnp.stack([out_grad] * lax.axis_size('head...  24.8 us
    rev x2, local copies, waits for them, and re-layouts, body(): reverse_sums = jnp.cumsum(pieces[1][::-1], 0)[::-1] - pieces[1]  15.9 us
    all_to_all x1, waiting for transfers between devices, body(): lax.all_to_all(stacked, 'seq', split_axis=1, concat_axis=1, tiled=True)  11.6 us
    all_to_all x1, starting transfers between devices, body(): lax.all_to_all(stacked, 'seq', split_axis=1, concat_axis=1, tiled=True)  11.4 us
    unnamed x31, local copies, waits for them, and re-layouts  9.97 us
    dot_general x1, matrix products, body(): jnp.einsum('tm,hdm->thd', jnp.concatenate(lax.all_to_all(jnp.stack([out_g...  8.29 us
    all_to_all x1, waiting for transfers between devices, body(): lax.all_to_all(jnp.stack([forward_sums, reverse_sums]), 'seq', split_axis...  7.76 us
  transfers between devices with their start and end apart: 3, of which 3 were waited for; matrix products, arithmetic and copies ran while one was open for 6% of the time, Pallas kernels for 0%

profile of v1, /device:TPU:32, one launch (start us, length us, event | category | flops | bytes accessed | tf_op | source)
XLA Modules:
  0.0 240.0 jit_solution(6791500627112123716)
XLA Ops:
  0.6 5.2 %stack.12 = bf16[8,1024,512]{2,1,0:T(8,128)(2,1)} broadcast(bf16[1024,512]{1,0:T(8,128)(2,1)} %param.8), dimensions={1,2} | broadcast | bytes 9437184 | tf_op jit(solution)/shard_map/stack | solution.py:19
  5.8 5.1 %all-to-all-start = ((bf16[8,1024,512]{2,1,0:T(8,128)(2,1)}), bf16[8,1024,512]{2,1,0:T(8,128)(2,1)}, u32[]{:S(2)}, u32[]{:S(2)}) async-start(bf16[8,1024,512]{2,1,0:T(8,128)(2,1)} %stack.12), calls=%async_computation | async-start | bytes 16777216 | tf_op jit(solution)/shard_map/all_to_all | solution.py:19
  12.2 93.3 %all-to-all-done = bf16[8,1024,512]{2,1,0:T(8,128)(2,1)} async-done(((bf16[8,1024,512]{2,1,0:T(8,128)(2,1)}), bf16[8,1024,512]{2,1,0:T(8,128)(2,1)}, u32[]{:S(2)}, u32[]{:S(2)}) %all-to-all-start) | async-done | bytes 8388640 | tf_op jit(solution)/shard_map/all_to_all | solution.py:19
  105.5 11.3 %copy.77 = bf16[1024,8,512]{2,1,0:T(8,128)(2,1)} copy(bf16[1024,8,512]{2,0,1:T(8,128)(2,1)} %bitcast) | data formatting | bytes 16777216 | tf_op jit(solution)/shard_map/reshape | solution.py:18
  116.8 13.5 %reshape.57 = bf16[1024,4096,1]{1,0,2:T(8,128)(2,1)} reshape(bf16[1024,8,512]{2,1,0:T(8,128)(2,1)} %copy.77) | data formatting | bytes 16777216 | tf_op jit(solution)/shard_map/reshape | solution.py:18
  130.3 8.3 %convolution_convert_fusion = bf16[1024,4,128]{2,0,1:T(8,128)(2,1)S(1)} fusion(bf16[1024,4096,1]{1,0,2:T(8,128)(2,1)} %reshape.57, bf16[4,128,4096]{2,1,0:T(8,128)(2,1)} %param.9), kind=kOutput, calls=%fused_computation.10 | convolution fusion | flops 4295491584 | bytes 13631488 | tf_op jit(solution)/shard_map/tm,hdm->thd/dot_general | solution.py:16
  144.0 11.4 %all-to-all-start.1 = ((f32[2,32,2048]{2,0,1:T(2,128)}), f32[2,32,2048]{2,0,1:T(2,128)}, u32[]{:S(2)}, u32[]{:S(2)}) async-start(f32[2,32,2048]{2,0,1:T(2,128)} %copy.86), calls=%async_computation.1 | async-start | bytes 1048576 | tf_op jit(solution)/shard_map/all_to_all | solution.py:39
  159.0 2.3 select_convert_fusion.1
  161.3 11.6 %all-to-all-done.1 = f32[2,32,2048]{2,0,1:T(2,128)} async-done(((f32[2,32,2048]{2,0,1:T(2,128)}), f32[2,32,2048]{2,0,1:T(2,128)}, u32[]{:S(2)}, u32[]{:S(2)}) %all-to-all-start.1) | async-done | bytes 524320 | tf_op jit(solution)/shard_map/all_to_all | solution.py:39
  176.1 1.9 reduce_window_sum.34
  178.0 1.8 copy_subtract_fusion
  180.6 7.9 %rev.10 = f32[32,2048]{1,0:T(8,128)} reverse(f32[32,2048]{1,0:T(8,128)} %bitcast.61), dimensions={0} | reverse | bytes 524288 | tf_op jit(solution)/shard_map/rev | solution.py:41
  188.5 1.9 reduce_window_sum.35
  190.4 7.9 %rev.11 = f32[32,2048]{1,0:T(8,128)} reverse(f32[32,2048]{1,0:T(8,128)} %reduce_window_sum.35), dimensions={0} | reverse | bytes 524288 | tf_op jit(solution)/shard_map/rev | solution.py:41
  201.6 4.9 %all-to-all-start.2 = ((f32[2,32,2048]{2,0,1:T(2,128)}), f32[2,32,2048]{2,0,1:T(2,128)}, u32[]{:S(2)}, u32[]{:S(2)}) async-start(f32[2,32,2048]{2,0,1:T(2,128)} %copy.89), calls=%async_computation.2 | async-start | bytes 1048576 | tf_op jit(solution)/shard_map/all_to_all | solution.py:42
  206.5 3.3 %fusion.8 = f32[4,4,256,128]{3,2,1,0:T(8,128)} fusion(bf16[4,4,256,256]{3,2,1,0:T(8,128)(2,1)S(1)} %select_convert_fusion.1, bf16[4,256,4,128]{3,2,1,0:T(4,128)(2,1)} %bitcast.47), kind=kOutput, calls=%fused_computation.16 | convolution fusion | flops 268435456 | bytes 5242880 | tf_op jit(solution)/shard_map/bhts,bthd->bshd/dot_general | solution.py:70
  209.8 2.0 fusion.19
  211.8 3.9 %fusion.4 = f32[4,4,128,256]{3,2,1,0:T(8,128)} fusion(pred[256,256]{1,0:T(8,128)(4,1)S(1)} %iota_compare_fusion, bf16[4,256,4,128]{3,2,1,0:T(4,128)(2,1)} %bitcast.48, bf16[4,256,4,128]{3,2,1,0:T(4,128)(2,1)S(1)} %bitcast.45, bf16[4,256,4,128]{3,1,0,2:T(8,128)(2,1)} %bitcast.55), kind=kOutput, calls=%fused_computation.9 | convolution fusion | flops 538968064 | bytes 5308416 | tf_op jit(solution)/shard_map/bhts,bthe->bshe/dot_general | solution.py:76
  215.7 7.8 %all-to-all-done.2 = f32[2,32,2048]{2,0,1:T(2,128)} async-done(((f32[2,32,2048]{2,0,1:T(2,128)}), f32[2,32,2048]{2,0,1:T(2,128)}, u32[]{:S(2)}, u32[]{:S(2)}) %all-to-all-start.2) | async-done | bytes 524320 | tf_op jit(solution)/shard_map/all_to_all | solution.py:42
  223.5 2.5 %fusion.30 = (f32[1,32,2048]{2,0,1:T(1,128)S(1)}, f32[1,32,2048]{2,0,1:T(1,128)}) fusion(f32[2,32,2048]{2,0,1:T(2,128)} %all-to-all-done.2), kind=kLoop, calls=%fused_computation.43 | loop fusion | bytes 1048576 | tf_op jit(solution)/shard_map/slice | solution.py:47
  226.1 3.0 %fusion.5 = bf16[4,256,4,128]{1,3,2,0:T(8,128)(2,1)} fusion(f32[4,4,128,256]{3,2,1,0:T(8,128)} %fusion.4, bf16[4,256,4,128]{3,2,1,0:T(4,128)(2,1)S(1)} %bitcast.46, f32[3,4,128,128]{2,3,1,0:T(8,128)S(1)} %copy-done.3, f32[4,128,128]{1,2,0:T(8,128)S(1)} %copy.95), kind=kOutput, calls=%fused_computation.11 | convolution fusion | flops 136314880 | bytes 5242880 | tf_op jit(solution)/shard_map/bshd,bhde->bshe/dot_general | solution.py:79
  229.1 2.4 %copy.104 = bf16[4,256,4,128]{3,1,0,2:T(8,128)(2,1)} copy(bf16[4,256,4,128]{1,3,2,0:T(8,128)(2,1)} %fusion.5) | data formatting | bytes 2097152 | tf_op jit(solution)/shard_map/convert_element_type | solution.py:86
  231.6 3.1 %copy.107 = bf16[1024,4,128]{2,1,0:T(4,128)(2,1)} copy(bf16[1024,4,128]{2,0,1:T(8,128)(2,1)} %bitcast.57) | data formatting | bytes 2097152
  235.3 1.8 copy.106
  (53 shorter events, 21.1 us)
Async XLA Ops:
  5.8 5.1 %copy-start = (bf16[1024,4,128]{2,1,0:T(4,128)(2,1)S(1)}, bf16[1024,4,128]{2,1,0:T(4,128)(2,1)}, u32[]{:S(2)}) copy-start(bf16[1024,4,128]{2,1,0:T(4,128)(2,1)} %param.6) | copy-start | bytes 3145732
  5.8 5.1 %copy-start.6 = (bf16[1024,4,128]{2,1,0:T(4,128)(2,1)S(1)}, bf16[1024,4,128]{2,1,0:T(4,128)(2,1)}, u32[]{:S(2)}) copy-start(bf16[1024,4,128]{2,1,0:T(4,128)(2,1)} %param.7) | copy-start | bytes 3145732
  5.8 99.7 %all-to-all-start = ((bf16[8,1024,512]{2,1,0:T(8,128)(2,1)}), bf16[8,1024,512]{2,1,0:T(8,128)(2,1)}, u32[]{:S(2)}, u32[]{:S(2)}) async-start(bf16[8,1024,512]{2,1,0:T(8,128)(2,1)} %stack.12), calls=%async_computation | async-start | bytes 16777216 | tf_op jit(solution)/shard_map/all_to_all | solution.py:19
  130.3 8.3 %copy-start.5 = (bf16[1024,4,128]{2,1,0:T(4,128)(2,1)S(1)}, bf16[1024,4,128]{2,1,0:T(4,128)(2,1)}, u32[]{:S(2)}) copy-start(bf16[1024,4,128]{2,1,0:T(4,128)(2,1)} %param.5) | copy-start | bytes 3145732
  138.6 1.2 copy-start.8
  144.0 28.9 %all-to-all-start.1 = ((f32[2,32,2048]{2,0,1:T(2,128)}), f32[2,32,2048]{2,0,1:T(2,128)}, u32[]{:S(2)}, u32[]{:S(2)}) async-start(f32[2,32,2048]{2,0,1:T(2,128)} %copy.86), calls=%async_computation.1 | async-start | bytes 1048576 | tf_op jit(solution)/shard_map/all_to_all | solution.py:39
  156.2 1.0 copy-start.10
  174.6 0.7 copy-start.11
  201.6 21.9 %all-to-all-start.2 = ((f32[2,32,2048]{2,0,1:T(2,128)}), f32[2,32,2048]{2,0,1:T(2,128)}, u32[]{:S(2)}, u32[]{:S(2)}) async-start(f32[2,32,2048]{2,0,1:T(2,128)} %copy.89), calls=%async_computation.2 | async-start | bytes 1048576 | tf_op jit(solution)/shard_map/all_to_all | solution.py:42
  215.7 10.4 %copy-start.3 = (f32[3,4,128,128]{2,3,1,0:T(8,128)S(1)}, f32[3,4,128,128]{2,3,1,0:T(8,128)}, u32[]{:S(2)}) copy-start(f32[3,4,128,128]{2,3,1,0:T(8,128)} %slice.31) | copy-start | bytes 2359300
  229.1 5.5 %copy-start.2 = (f32[4,4,256,128]{3,2,1,0:T(8,128)S(1)}, f32[4,4,256,128]{3,2,1,0:T(8,128)}, u32[]{:S(2)}) copy-start(f32[4,4,256,128]{3,2,1,0:T(8,128)} %fusion.8) | copy-start | bytes 6291460
  229.1 5.5 %copy-start.4 = (f32[3,4,128,128]{2,3,1,0:T(8,128)S(1)}, f32[3,4,128,128]{2,3,1,0:T(8,128)}, u32[]{:S(2)}) copy-start(f32[3,4,128,128]{2,3,1,0:T(8,128)} %slice.31) | copy-start | bytes 2359300
  231.6 3.1 %copy-start.7 = (bf16[1024,4,128]{2,1,0:T(4,128)(2,1)S(1)}, bf16[1024,4,128]{2,1,0:T(4,128)(2,1)}, u32[]{:S(2)}) copy-start(bf16[1024,4,128]{2,1,0:T(4,128)(2,1)} %param.7) | copy-start | bytes 3145732
  235.2 1.9 copy-start.1
  235.2 1.9 copy-start.9
  235.2 2.4 %slice-start = ((f32[4,4,128,128]{3,2,1,0:T(8,128)}), f32[3,4,128,128]{3,2,1,0:T(8,128)S(1)}, s32[]{:S(2)}) async-start(f32[4,4,128,128]{3,2,1,0:T(8,128)} %copy-done.10), calls=%async_computation.3 | async-start | bytes 1572864 | tf_op jit(solution)/shard_map/slice | solution.py:50
  235.2 2.5 %copy-start.12 = (f32[1,32,2048]{2,0,1:T(1,128)S(1)}, f32[1,32,2048]{2,0,1:T(1,128)}, u32[]{:S(2)}) copy-start(f32[1,32,2048]{2,0,1:T(1,128)} %get-tuple-element.13) | copy-start | bytes 786436
